TPU v7x, 32 devices: a whole 2x2x4 slice. The times are simulated.
32 devices in a mesh: grp: 8 (over y, x, core), sh: 4 (over z).
Axes of the slice: x: 2, y: 2, z: 4, core: 2. Of those that a mesh axis runs over, the one named last changes fastest.
Arguments:
- factors: bfloat16 [24, 128, 14336], P('grp', None, 'sh'), may hold values from -0.5 to 0.5
- screen: int32 [24, 1, 112], P('grp', None, 'sh'), may hold values 0 or 1
- occ_energy: float32 [24], replicated, may hold values from -1.5 to -0.3
- virt_energy: float32 [128], replicated, may hold values from 0.5 to 3
Outputs:
- gamma: bfloat16 [24, 128, 14336], P('grp', 'sh')
Inputs may be any that keep to these rules, and one draw needn't show every extreme that they name: `screen`: 1 keeps a block of 128 virtual by 128 auxiliary functions of one occupied orbital, 0 screens it out.
All inputs are finite; a program needn't handle non-finite values.
Results may differ from a plain program's by a relative error of at most 0.0049.
Values may be sent and summed in bfloat16 or wider, within the bound.
A program may use at most 64 MiB of HBM per device.

v0:
```python
import jax
import jax.numpy as jnp
from jax import lax
from jax.sharding import PartitionSpec as P

BLK = 128


def passed_along(value, axis, steps):
    count = lax.axis_size(axis)
    pairs = [(source, (source + steps) % count) for source in range(count)]
    return lax.ppermute(value, axis, pairs)


def on_device(factors, screen, occ_energy, virt_energy):
    occ_g, virt_width, aux_dev = factors.shape
    row_count = occ_g * virt_width
    groups = lax.axis_size("grp")
    shards = lax.axis_size("sh")
    slice_rows = row_count // shards
    my_group = lax.axis_index("grp")
    wide_mask = jnp.repeat(jnp.repeat(screen, BLK, axis=1), BLK, axis=2)
    own_block = (factors * wide_mask.astype(jnp.bfloat16)).reshape(row_count, aux_dev)
    occ_own = lax.dynamic_slice_in_dim(occ_energy, my_group * occ_g, occ_g)
    all_rows = (virt_energy[None, :] - occ_own[:, None]).reshape(-1)
    row_energy = lax.dynamic_slice_in_dim(all_rows, lax.axis_index("sh") * slice_rows, slice_rows)

    def update(running, partner, other_group):
        occ_other = lax.dynamic_slice_in_dim(occ_energy, other_group * occ_g, occ_g)
        col_energy = (virt_energy[None, :] - occ_other[:, None]).reshape(-1)
        coulomb = lax.psum_scatter(
            lax.dot_general(
                own_block, partner, (((1,), (1,)), ((), ())), preferred_element_type=jnp.float32
            ),
            "sh",
            scatter_dimension=0,
            tiled=True,
        )
        amplitude = (coulomb / (row_energy[:, None] + col_energy[None, :])).astype(jnp.bfloat16)
        full_amp = lax.all_gather(amplitude, "sh", axis=0, tiled=True)
        four_index = full_amp.reshape(occ_g, virt_width, occ_g, virt_width).astype(jnp.float32)
        combined = (2.0 * four_index - jnp.transpose(four_index, (0, 3, 2, 1))).astype(jnp.bfloat16)
        combined = combined.reshape(row_count, row_count)
        return running + jnp.dot(combined, partner, preferred_element_type=jnp.float32)

    gamma_sum = update(jnp.zeros((row_count, aux_dev), jnp.float32), own_block, my_group)

    def one_turn(turn_index, state_tuple):
        running, partner = state_tuple
        partner = passed_along(partner, "grp", 1)
        return (update(running, partner, (my_group - turn_index) % groups), partner)

    gamma_sum, moved = lax.fori_loop(1, groups, one_turn, (gamma_sum, own_block))
    gamma_local = gamma_sum.astype(jnp.bfloat16).reshape(occ_g, virt_width, aux_dev)
    return lax.all_to_all(gamma_local, "sh", split_axis=1, concat_axis=2, tiled=True)


def solution(mesh):
    placed = (P("grp", None, "sh"), P("grp", None, "sh"), P(), P())
    return jax.shard_map(
        on_device, mesh=mesh, in_specs=placed, out_specs=P("grp", "sh", None), check_vma=False
    )
```

profile of v0, /device:TPU:0, one launch (start us, length us, event | category | flops | bytes accessed | tf_op | source)
XLA Modules:
  0.0 748.2 jit_solution(326986928586050484)
XLA Ops:
  7.3 3.5 broadcast_multiply_fusion
  10.8 5.0 fusion.8
  15.9 3.5 copy.71
  19.7 21.1 %reduce-scatter.3.cloned.1.call-done = f32[96,384]{1,0:T(8,128)} async-done(((f32[384,384]{1,0:T(8,128)}), f32[96,384]{1,0:T(8,128)}) %reduce-scatter.3.cloned.1.call-update) | async-done | bytes 147472 | tf_op jit(solution)/shard_map/reduce_scatter | solution.py:31
  41.8 14.4 %all_gather.13 = bf16[384,384]{1,0:T(8,128)(2,1)S(1)} all-gather(bf16[96,384]{1,0:T(8,128)(2,1)S(1)} %divide_convert_fusion.1), channel_id=1, replica_groups=mesh['grp'=8,'sh'=4] {'sh'}, dimensions={0}, use_global_device_ids=true | all-gather | bytes 368640 | tf_op jit(solution)/shard_map/all_gather | solution.py:40
  57.0 5.8 fusion.4
  62.7 590.5 %while.17 = (s32[]{:T(128)}, f32[384,3584]{1,0:T(8,128)}, bf16[384,3584]{1,0:T(8,128)(2,1)}, bf16[384,3584]{1,0:T(8,128)(2,1)}, f32[96]{0:T(128)S(1)}, /*index=5...) while((s32[]{:T(128)}, f32[384,3584]{1,0:T(8,128)}, ...), condition=%wide.region_3.4_spmd, body=%wide.region_1.3_spmd.sunk | while | flops 2115858816 | bytes 43602204 | solution.py:53
  62.7 33.6 %collective-permute-done = bf16[384,3584]{1,0:T(8,128)(2,1)S(1)} collective-permute-done((bf16[384,3584]{1,0:T(8,128)(2,1)}, bf16[384,3584]{1,0:T(8,128)(2,1)S(1)}, u32[]{:S(2)}, u32[]{:S(2)}) %collective-permute-start) | collective-permute-done | bytes 2752544 | tf_op jit(solution)/shard_map/while/body/eval_jaxpr/ppermute | solution.py:12
  96.3 4.2 fusion.25
  100.8 1.5 copy.77
  102.3 18.2 %reduce-scatter.5.cloned.1.call-done = f32[96,384]{1,0:T(8,128)} async-done(((f32[384,384]{1,0:T(8,128)}), f32[96,384]{1,0:T(8,128)}) %reduce-scatter.5.cloned.1.call-update) | async-done | bytes 147472 | tf_op jit(solution)/shard_map/while/body/eval_jaxpr/reduce_scatter | solution.py:31
  121.5 15.3 %all_gather.15 = bf16[384,384]{1,0:T(8,128)(2,1)} all-gather(bf16[96,384]{1,0:T(8,128)(2,1)S(1)} %divide_convert_fusion.3), channel_id=1, replica_groups=mesh['grp'=8,'sh'=4] {'sh'}, dimensions={0}, use_global_device_ids=true | all-gather | bytes 368640 | tf_op jit(solution)/shard_map/while/body/eval_jaxpr/all_gather | solution.py:40
  140.6 6.5 convolution_add_fusion.2
  147.2 33.6 %collective-permute-done = bf16[384,3584]{1,0:T(8,128)(2,1)S(1)} collective-permute-done((bf16[384,3584]{1,0:T(8,128)(2,1)}, bf16[384,3584]{1,0:T(8,128)(2,1)S(1)}, u32[]{:S(2)}, u32[]{:S(2)}) %collective-permute-start) | collective-permute-done | bytes 2752544 | tf_op jit(solution)/shard_map/while/body/eval_jaxpr/ppermute | solution.py:12
  180.8 4.2 fusion.25
  185.2 1.5 copy.77
  186.8 17.9 %reduce-scatter.5.cloned.1.call-done = f32[96,384]{1,0:T(8,128)} async-done(((f32[384,384]{1,0:T(8,128)}), f32[96,384]{1,0:T(8,128)}) %reduce-scatter.5.cloned.1.call-update) | async-done | bytes 147472 | tf_op jit(solution)/shard_map/while/body/eval_jaxpr/reduce_scatter | solution.py:31
  205.7 15.3 %all_gather.15 = bf16[384,384]{1,0:T(8,128)(2,1)} all-gather(bf16[96,384]{1,0:T(8,128)(2,1)S(1)} %divide_convert_fusion.3), channel_id=1, replica_groups=mesh['grp'=8,'sh'=4] {'sh'}, dimensions={0}, use_global_device_ids=true | all-gather | bytes 368640 | tf_op jit(solution)/shard_map/while/body/eval_jaxpr/all_gather | solution.py:40
  224.9 6.6 convolution_add_fusion.2
  231.4 33.6 %collective-permute-done = bf16[384,3584]{1,0:T(8,128)(2,1)S(1)} collective-permute-done((bf16[384,3584]{1,0:T(8,128)(2,1)}, bf16[384,3584]{1,0:T(8,128)(2,1)S(1)}, u32[]{:S(2)}, u32[]{:S(2)}) %collective-permute-start) | collective-permute-done | bytes 2752544 | tf_op jit(solution)/shard_map/while/body/eval_jaxpr/ppermute | solution.py:12
  265.0 4.2 fusion.25
  271.0 18.1 %reduce-scatter.5.cloned.1.call-done = f32[96,384]{1,0:T(8,128)} async-done(((f32[384,384]{1,0:T(8,128)}), f32[96,384]{1,0:T(8,128)}) %reduce-scatter.5.cloned.1.call-update) | async-done | bytes 147472 | tf_op jit(solution)/shard_map/while/body/eval_jaxpr/reduce_scatter | solution.py:31
  290.1 15.3 %all_gather.15 = bf16[384,384]{1,0:T(8,128)(2,1)} all-gather(bf16[96,384]{1,0:T(8,128)(2,1)S(1)} %divide_convert_fusion.3), channel_id=1, replica_groups=mesh['grp'=8,'sh'=4] {'sh'}, dimensions={0}, use_global_device_ids=true | all-gather | bytes 368640 | tf_op jit(solution)/shard_map/while/body/eval_jaxpr/all_gather | solution.py:40
  309.2 6.5 convolution_add_fusion.2
  315.8 33.6 %collective-permute-done = bf16[384,3584]{1,0:T(8,128)(2,1)S(1)} collective-permute-done((bf16[384,3584]{1,0:T(8,128)(2,1)}, bf16[384,3584]{1,0:T(8,128)(2,1)S(1)}, u32[]{:S(2)}, u32[]{:S(2)}) %collective-permute-start) | collective-permute-done | bytes 2752544 | tf_op jit(solution)/shard_map/while/body/eval_jaxpr/ppermute | solution.py:12
  349.4 4.2 fusion.25
  355.4 18.1 %reduce-scatter.5.cloned.1.call-done = f32[96,384]{1,0:T(8,128)} async-done(((f32[384,384]{1,0:T(8,128)}), f32[96,384]{1,0:T(8,128)}) %reduce-scatter.5.cloned.1.call-update) | async-done | bytes 147472 | tf_op jit(solution)/shard_map/while/body/eval_jaxpr/reduce_scatter | solution.py:31
  374.5 15.4 %all_gather.15 = bf16[384,384]{1,0:T(8,128)(2,1)} all-gather(bf16[96,384]{1,0:T(8,128)(2,1)S(1)} %divide_convert_fusion.3), channel_id=1, replica_groups=mesh['grp'=8,'sh'=4] {'sh'}, dimensions={0}, use_global_device_ids=true | all-gather | bytes 368640 | tf_op jit(solution)/shard_map/while/body/eval_jaxpr/all_gather | solution.py:40
  393.7 6.5 convolution_add_fusion.2
  400.2 33.6 %collective-permute-done = bf16[384,3584]{1,0:T(8,128)(2,1)S(1)} collective-permute-done((bf16[384,3584]{1,0:T(8,128)(2,1)}, bf16[384,3584]{1,0:T(8,128)(2,1)S(1)}, u32[]{:S(2)}, u32[]{:S(2)}) %collective-permute-start) | collective-permute-done | bytes 2752544 | tf_op jit(solution)/shard_map/while/body/eval_jaxpr/ppermute | solution.py:12
  433.8 4.2 fusion.25
  439.8 17.9 %reduce-scatter.5.cloned.1.call-done = f32[96,384]{1,0:T(8,128)} async-done(((f32[384,384]{1,0:T(8,128)}), f32[96,384]{1,0:T(8,128)}) %reduce-scatter.5.cloned.1.call-update) | async-done | bytes 147472 | tf_op jit(solution)/shard_map/while/body/eval_jaxpr/reduce_scatter | solution.py:31
  458.7 15.3 %all_gather.15 = bf16[384,384]{1,0:T(8,128)(2,1)} all-gather(bf16[96,384]{1,0:T(8,128)(2,1)S(1)} %divide_convert_fusion.3), channel_id=1, replica_groups=mesh['grp'=8,'sh'=4] {'sh'}, dimensions={0}, use_global_device_ids=true | all-gather | bytes 368640 | tf_op jit(solution)/shard_map/while/body/eval_jaxpr/all_gather | solution.py:40
  477.8 6.5 convolution_add_fusion.2
  484.4 33.6 %collective-permute-done = bf16[384,3584]{1,0:T(8,128)(2,1)S(1)} collective-permute-done((bf16[384,3584]{1,0:T(8,128)(2,1)}, bf16[384,3584]{1,0:T(8,128)(2,1)S(1)}, u32[]{:S(2)}, u32[]{:S(2)}) %collective-permute-start) | collective-permute-done | bytes 2752544 | tf_op jit(solution)/shard_map/while/body/eval_jaxpr/ppermute | solution.py:12
  518.0 4.2 fusion.25
  524.0 18.1 %reduce-scatter.5.cloned.1.call-done = f32[96,384]{1,0:T(8,128)} async-done(((f32[384,384]{1,0:T(8,128)}), f32[96,384]{1,0:T(8,128)}) %reduce-scatter.5.cloned.1.call-update) | async-done | bytes 147472 | tf_op jit(solution)/shard_map/while/body/eval_jaxpr/reduce_scatter | solution.py:31
  543.1 15.3 %all_gather.15 = bf16[384,384]{1,0:T(8,128)(2,1)} all-gather(bf16[96,384]{1,0:T(8,128)(2,1)S(1)} %divide_convert_fusion.3), channel_id=1, replica_groups=mesh['grp'=8,'sh'=4] {'sh'}, dimensions={0}, use_global_device_ids=true | all-gather | bytes 368640 | tf_op jit(solution)/shard_map/while/body/eval_jaxpr/all_gather | solution.py:40
  562.2 6.5 convolution_add_fusion.2
  568.8 33.6 %collective-permute-done = bf16[384,3584]{1,0:T(8,128)(2,1)S(1)} collective-permute-done((bf16[384,3584]{1,0:T(8,128)(2,1)}, bf16[384,3584]{1,0:T(8,128)(2,1)S(1)}, u32[]{:S(2)}, u32[]{:S(2)}) %collective-permute-start) | collective-permute-done | bytes 2752544 | tf_op jit(solution)/shard_map/while/body/eval_jaxpr/ppermute | solution.py:12
  602.4 4.2 fusion.25
  608.4 18.2 %reduce-scatter.5.cloned.1.call-done = f32[96,384]{1,0:T(8,128)} async-done(((f32[384,384]{1,0:T(8,128)}), f32[96,384]{1,0:T(8,128)}) %reduce-scatter.5.cloned.1.call-update) | async-done | bytes 147472 | tf_op jit(solution)/shard_map/while/body/eval_jaxpr/reduce_scatter | solution.py:31
  627.5 15.3 %all_gather.15 = bf16[384,384]{1,0:T(8,128)(2,1)} all-gather(bf16[96,384]{1,0:T(8,128)(2,1)S(1)} %divide_convert_fusion.3), channel_id=1, replica_groups=mesh['grp'=8,'sh'=4] {'sh'}, dimensions={0}, use_global_device_ids=true | all-gather | bytes 368640 | tf_op jit(solution)/shard_map/while/body/eval_jaxpr/all_gather | solution.py:40
  646.7 6.5 convolution_add_fusion.2
  653.2 2.8 convert_element_type.66
  656.1 2.4 copy.35
  658.5 80.5 %all_to_all.18 = bf16[3,128,3584]{2,0,1:T(4,128)(2,1)S(1)} all-to-all(bf16[3,128,3584]{2,0,1:T(4,128)(2,1)S(1)} %copy.35), channel_id=1, replica_groups=mesh['grp'=8,'sh'=4] {'sh'}, dimensions={1} | all-to-all | bytes 5505024 | tf_op jit(solution)/shard_map/all_to_all | solution.py:55
  739.6 1.8 copy.40
  (94 shorter events, 45.9 us)
Async XLA Ops:
  6.5 34.2 %reduce-scatter.3.cloned.1.call-start = ((), (), s32[]{:S(2)}) async-start(), calls=%async_computation.3 | async-start | bytes 737280 | tf_op jit(solution)/shard_map/reduce_scatter | solution.py:31
  15.9 3.5 copy-start.1
  15.9 3.6 copy-start
  62.7 57.7 %reduce-scatter.5.cloned.1.call-start = ((), (), s32[]{:S(2)}) async-start(), calls=%async_computation.4 | async-start | bytes 737280 | tf_op jit(solution)/shard_map/while/body/eval_jaxpr/reduce_scatter | solution.py:31
  62.7 33.6 %collective-permute-start = (bf16[384,3584]{1,0:T(8,128)(2,1)}, bf16[384,3584]{1,0:T(8,128)(2,1)S(1)}, u32[]{:S(2)}, u32[]{:S(2)}) collective-permute-start(bf16[384,3584]{1,0:T(8,128)(2,1)} %get-tuple-element.286), channel_id=1, source_target_pairs={{0,4},{4,8},{8,12},{12,16},{16,20},{20,24},{24,28},{28,0},{1,5},{5... | collective-permute-start | bytes 8257544 | tf_op jit(solution)/shard_map/while/body/eval_jaxpr/ppermute | solution.py:12
  147.2 57.5 %reduce-scatter.5.cloned.1.call-start = ((), (), s32[]{:S(2)}) async-start(), calls=%async_computation.4 | async-start | bytes 737280 | tf_op jit(solution)/shard_map/while/body/eval_jaxpr/reduce_scatter | solution.py:31
  147.2 33.6 %collective-permute-start = (bf16[384,3584]{1,0:T(8,128)(2,1)}, bf16[384,3584]{1,0:T(8,128)(2,1)S(1)}, u32[]{:S(2)}, u32[]{:S(2)}) collective-permute-start(bf16[384,3584]{1,0:T(8,128)(2,1)} %get-tuple-element.286), channel_id=1, source_target_pairs={{0,4},{4,8},{8,12},{12,16},{16,20},{20,24},{24,28},{28,0},{1,5},{5... | collective-permute-start | bytes 8257544 | tf_op jit(solution)/shard_map/while/body/eval_jaxpr/ppermute | solution.py:12
  231.4 57.7 %reduce-scatter.5.cloned.1.call-start = ((), (), s32[]{:S(2)}) async-start(), calls=%async_computation.4 | async-start | bytes 737280 | tf_op jit(solution)/shard_map/while/body/eval_jaxpr/reduce_scatter | solution.py:31
  231.4 33.6 %collective-permute-start = (bf16[384,3584]{1,0:T(8,128)(2,1)}, bf16[384,3584]{1,0:T(8,128)(2,1)S(1)}, u32[]{:S(2)}, u32[]{:S(2)}) collective-permute-start(bf16[384,3584]{1,0:T(8,128)(2,1)} %get-tuple-element.286), channel_id=1, source_target_pairs={{0,4},{4,8},{8,12},{12,16},{16,20},{20,24},{24,28},{28,0},{1,5},{5... | collective-permute-start | bytes 8257544 | tf_op jit(solution)/shard_map/while/body/eval_jaxpr/ppermute | solution.py:12
  315.8 57.7 %reduce-scatter.5.cloned.1.call-start = ((), (), s32[]{:S(2)}) async-start(), calls=%async_computation.4 | async-start | bytes 737280 | tf_op jit(solution)/shard_map/while/body/eval_jaxpr/reduce_scatter | solution.py:31
  315.8 33.6 %collective-permute-start = (bf16[384,3584]{1,0:T(8,128)(2,1)}, bf16[384,3584]{1,0:T(8,128)(2,1)S(1)}, u32[]{:S(2)}, u32[]{:S(2)}) collective-permute-start(bf16[384,3584]{1,0:T(8,128)(2,1)} %get-tuple-element.286), channel_id=1, source_target_pairs={{0,4},{4,8},{8,12},{12,16},{16,20},{20,24},{24,28},{28,0},{1,5},{5... | collective-permute-start | bytes 8257544 | tf_op jit(solution)/shard_map/while/body/eval_jaxpr/ppermute | solution.py:12
  400.2 57.5 %reduce-scatter.5.cloned.1.call-start = ((), (), s32[]{:S(2)}) async-start(), calls=%async_computation.4 | async-start | bytes 737280 | tf_op jit(solution)/shard_map/while/body/eval_jaxpr/reduce_scatter | solution.py:31
  400.2 33.6 %collective-permute-start = (bf16[384,3584]{1,0:T(8,128)(2,1)}, bf16[384,3584]{1,0:T(8,128)(2,1)S(1)}, u32[]{:S(2)}, u32[]{:S(2)}) collective-permute-start(bf16[384,3584]{1,0:T(8,128)(2,1)} %get-tuple-element.286), channel_id=1, source_target_pairs={{0,4},{4,8},{8,12},{12,16},{16,20},{20,24},{24,28},{28,0},{1,5},{5... | collective-permute-start | bytes 8257544 | tf_op jit(solution)/shard_map/while/body/eval_jaxpr/ppermute | solution.py:12
  484.4 57.7 %reduce-scatter.5.cloned.1.call-start = ((), (), s32[]{:S(2)}) async-start(), calls=%async_computation.4 | async-start | bytes 737280 | tf_op jit(solution)/shard_map/while/body/eval_jaxpr/reduce_scatter | solution.py:31
  484.4 33.6 %collective-permute-start = (bf16[384,3584]{1,0:T(8,128)(2,1)}, bf16[384,3584]{1,0:T(8,128)(2,1)S(1)}, u32[]{:S(2)}, u32[]{:S(2)}) collective-permute-start(bf16[384,3584]{1,0:T(8,128)(2,1)} %get-tuple-element.286), channel_id=1, source_target_pairs={{0,4},{4,8},{8,12},{12,16},{16,20},{20,24},{24,28},{28,0},{1,5},{5... | collective-permute-start | bytes 8257544 | tf_op jit(solution)/shard_map/while/body/eval_jaxpr/ppermute | solution.py:12
  568.8 57.7 %reduce-scatter.5.cloned.1.call-start = ((), (), s32[]{:S(2)}) async-start(), calls=%async_computation.4 | async-start | bytes 737280 | tf_op jit(solution)/shard_map/while/body/eval_jaxpr/reduce_scatter | solution.py:31
  568.8 33.6 %collective-permute-start = (bf16[384,3584]{1,0:T(8,128)(2,1)}, bf16[384,3584]{1,0:T(8,128)(2,1)S(1)}, u32[]{:S(2)}, u32[]{:S(2)}) collective-permute-start(bf16[384,3584]{1,0:T(8,128)(2,1)} %get-tuple-element.286), channel_id=1, source_target_pairs={{0,4},{4,8},{8,12},{12,16},{16,20},{20,24},{24,28},{28,0},{1,5},{5... | collective-permute-start | bytes 8257544 | tf_op jit(solution)/shard_map/while/body/eval_jaxpr/ppermute | solution.py:12
Sparse Core Ops, SparseCore 0:
  16.0 24.6 reduce-scatter.2
  100.7 19.7 reduce-scatter.4
  185.2 19.4 reduce-scatter.4
  269.4 19.6 reduce-scatter.4
  353.8 19.6 reduce-scatter.4
  438.2 19.4 reduce-scatter.4
  522.4 19.6 reduce-scatter.4
  606.8 19.7 reduce-scatter.4
where the time goes:
time: 750 us; the launch traced here: 748 us
  waiting for transfers between devices  383 us (51%)
  blocking collectives  202 us (27%)
  matrix products  86.3 us (12%)
  local copies, waits for them, and re-layouts  39.1 us (5%)
  other arithmetic  23.7 us (3%)
  between operations  13.5 us (2%)
    ppermute x7, waiting for transfers between devices, passed_along(): return lax.ppermute(value, axis, pairs)  235 us
    reduce_scatter x8, waiting for transfers between devices, update(): lax.psum_scatter(lax.dot_general(own_block, partner, (((1,), (1,)), ((),...  147 us
    all_gather x8, blocking collectives, update(): full_amp = lax.all_gather(amplitude, 'sh', axis=0, tiled=True)  122 us
    all_to_all x1, blocking collectives, on_device(): lax.all_to_all(gamma_local, 'sh', split_axis=1, concat_axis=2, tiled=True)  80.5 us
    dot_general x8, matrix products, update(): jnp.dot(combined, partner, preferred_element_type=jnp.float32)  51.6 us
    dot_general x8, matrix products, update(): lax.dot_general(own_block, partner, (((1,), (1,)), ((), ())), preferred_e...  34.7 us
    convert_element_type x16, local copies, waits for them, and re-layouts, update(): full_amp.reshape(occ_g, virt_width, occ_g, virt_width).astype(jnp.float32)  17.3 us
  transfers between devices with their start and end apart: 15, of which 15 were waited for; matrix products, arithmetic and copies ran while one was open for 2% of the time, Pallas kernels for 0%

commit v1 on v0

v1 whole, which is shorter than its diff:
```python
import functools

import jax
import jax.numpy as jnp
from jax import lax
from jax.experimental import pallas as pl
from jax.experimental.pallas import tpu as pltpu
from jax.sharding import PartitionSpec as P

BLK = 128
MESH = pl.DeviceIdType.MESH


def amplitude_kernel(
    dims, own_hbm, own_energy, all_energy, out, blocks, own_t, part32, part16, arrived, amp, tile32, weight, staged,
    own_sem, ring_send, ring_recv, twin_send, twin_recv, part_send, part_recv, amp_send, amp_recv, out_send, out_recv,
    out_local,
):
    occ_g, virt, aux, groups, shards = dims
    rows = occ_g * virt
    piece = rows // 2
    share = piece // shards
    slab = virt // shards
    chips = groups // 2
    span = chips // 2
    me_g, me_z = lax.axis_index("grp"), lax.axis_index("sh")
    core = lax.rem(me_g, 2)
    chip = lax.div(me_g, 2)
    odd, line = lax.rem(chip, 2), lax.div(chip, 2)
    spot = line + odd * (chips - 1 - 2 * line)

    def at(offset, other):
        place = lax.rem(spot + offset + chips, chips)
        that = 2 * place + lax.div(place, span) * (2 * chips - 1 - 4 * place)
        return 2 * that + (1 - core if other else core)

    def rows_of(offset, other, half):
        return pl.ds(pl.multiple_of((2 * at(offset, other) + half) * piece, piece), piece)

    right, left, twin = at(1, False), at(-1, False), at(0, True)
    peers = [lax.rem(me_z + q, shards) for q in range(1, shards)]
    before = [lax.rem(me_z - q + shards, shards) for q in range(1, shards)]

    load = pltpu.make_async_copy(own_hbm, blocks.at[pl.ds(pl.multiple_of(me_g * rows, rows), rows)], own_sem)
    load.start()
    barrier = pltpu.get_barrier_semaphore()
    for g in (right, left, twin):
        pl.semaphore_signal(barrier, inc=1, device_id=(g, me_z), device_id_type=MESH)
    for z in peers:
        pl.semaphore_signal(barrier, inc=1, device_id=(me_g, z), device_id_type=MESH)
    pl.semaphore_wait(barrier, 3 + shards - 1)
    load.wait()

    sent = []

    def ring(way, step, half):
        back = -(step - 1) if way == 0 else step - 1
        where = rows_of(back, False, half)
        return pltpu.make_async_remote_copy(
            src_ref=blocks.at[where], dst_ref=blocks.at[where],
            send_sem=ring_send.at[way, step - 1, half], recv_sem=ring_recv.at[way, step - 1, half],
            device_id=(right if way == 0 else left, me_z), device_id_type=MESH,
        )

    def ring_in(way, step, half):
        where = rows_of(-step if way == 0 else step, False, half)
        return pltpu.make_async_remote_copy(
            src_ref=blocks.at[where], dst_ref=blocks.at[where],
            send_sem=ring_send.at[way, step - 1, half], recv_sem=ring_recv.at[way, step - 1, half],
            device_id=(right if way == 0 else left, me_z), device_id_type=MESH,
        )

    def to_twin(offset, other, half, index):
        where = rows_of(offset, other, half)
        return pltpu.make_async_remote_copy(
            src_ref=blocks.at[where], dst_ref=blocks.at[where],
            send_sem=twin_send.at[index], recv_sem=twin_recv.at[index],
            device_id=(twin, me_z), device_id_type=MESH,
        )

    def go(copy):
        copy.start()
        sent.append(copy)

    halves = lambda way, step: ((0, 1) if way == 0 else (1, 0)) if step < span else ((0,) if way == 0 else (1,))

    for turn in range(2):
        for way in (0, 1):
            if turn < len(halves(way, 1)):
                go(ring(way, 1, halves(way, 1)[turn]))
    for half in (0, 1):
        go(to_twin(0, False, half, half))

    depth = BLK * 4 if aux % (BLK * 4) == 0 else BLK
    own_rows = pl.ds(pl.multiple_of(me_g * rows, rows), rows)

    @pl.loop(0, aux // depth)
    def _(k):
        at_k = pl.ds(pl.multiple_of(k * depth, depth), depth)
        own_t[at_k, :] = blocks[own_rows, at_k].astype(jnp.float32).T.astype(jnp.bfloat16)

    batches = [[(0, 0, None, 0, 0), (0, 1, None, 0, 1)]]
    index = 2
    for step in range(1, span + 1):
        for turn in range(len(halves(0, step))):
            batch = []
            for way in (0, 1):
                half = halves(way, step)[turn]
                batch.append((-step if way == 0 else step, half, way, step, index))
                index += 1
            batches.append(batch)

    def product(where, index):
        part32[...] = jnp.zeros_like(part32)

        @pl.loop(0, aux // depth)
        def _(k):
            at_k = pl.ds(pl.multiple_of(k * depth, depth), depth)
            part32[...] += jnp.dot(blocks[where, at_k], own_t[at_k, :], preferred_element_type=jnp.float32)

        for q in range(shards):
            part16[index, q] = part32[q * share:(q + 1) * share, :].astype(jnp.bfloat16)
        for q, z in enumerate(peers):
            go(pltpu.make_async_remote_copy(
                src_ref=part16.at[index, z], dst_ref=arrived.at[index, q],
                send_sem=part_send.at[index, q], recv_sem=part_recv.at[index, q],
                device_id=(me_g, z), device_id_type=MESH,
            ))

    def divide(offset, other, half, index):
        total = part16[index, me_z].astype(jnp.float32)
        for q in range(shards - 1):
            pltpu.make_async_copy(arrived.at[index, q], arrived.at[index, q], part_recv.at[index, q]).wait()
            total += arrived[index, q].astype(jnp.float32)
        gap = all_energy[2 * at(offset, other) + half, me_z] + own_energy[...]
        amp[index, me_z] = (total / gap).astype(jnp.bfloat16)
        for q, z in enumerate(peers):
            go(pltpu.make_async_remote_copy(
                src_ref=amp.at[index, me_z], dst_ref=amp.at[index, me_z],
                send_sem=amp_send.at[index, q], recv_sem=amp_recv.at[index, q],
                device_id=(me_g, z), device_id_type=MESH,
            ))

    def combine(offset, other, indices):
        for half in (0, 1):
            for q, z in enumerate(before):
                slot = amp.at[indices[half], z]
                pltpu.make_async_copy(slot, slot, amp_recv.at[indices[half], q]).wait()
            for q in range(shards):
                low = half * piece + q * share
                tile32[low:low + share, :] = amp[indices[half], q].astype(jnp.float32)
        first = at(offset, other) * rows
        for j in range(occ_g):
            columns = pl.ds(pl.multiple_of(first + j * virt, virt), virt)
            for i in range(occ_g):
                tile = tile32[j * virt:(j + 1) * virt, i * virt:(i + 1) * virt]
                weight[i * virt:(i + 1) * virt, columns] = (2.0 * tile.T - tile).astype(jnp.bfloat16)

    seen = {}
    ready = []
    for batch in batches:
        work = []
        for offset, half, way, step, index in batch:
            if way is not None:
                ring_in(way, step, half).wait_recv()
                if step < span and half in halves(way, step + 1):
                    go(ring(way, step + 1, half))
                go(to_twin(offset, False, half, index))
            work.append((offset, False, half, 2 * index))
        for offset, other, half, index in work:
            product(rows_of(offset, other, half), index)
        for offset, half, way, step, index in batch:
            to_twin(offset, True, half, index).wait_recv()
            product(rows_of(offset, True, half), 2 * index + 1)
            work.append((offset, True, half, 2 * index + 1))
        for entry in work:
            divide(*entry)
        for entry in ready:
            combine(*entry)
        ready = []
        for offset, other, half, index in work:
            key = (offset % chips, other)
            seen.setdefault(key, {})[half] = index
            if len(seen[key]) == 2:
                ready.append((offset, other, seen[key]))
    for entry in ready:
        combine(*entry)

    wide = depth
    turns = aux // wide

    def out_copy(c, q, z, source):
        return pltpu.make_async_remote_copy(
            src_ref=staged.at[z, :, :, pl.ds(pl.multiple_of(c * wide, wide), wide)],
            dst_ref=out.at[:, :, pl.ds(pl.multiple_of(source * aux + c * wide, wide), wide)],
            send_sem=out_send.at[c, q], recv_sem=out_recv.at[c, q],
            device_id=(me_g, z), device_id_type=MESH,
        )

    def out_own(c):
        return pltpu.make_async_copy(
            staged.at[me_z, :, :, pl.ds(pl.multiple_of(c * wide, wide), wide)],
            out.at[:, :, pl.ds(pl.multiple_of(me_z * aux + c * wide, wide), wide)],
            out_local.at[c],
        )

    @pl.loop(0, turns)
    def _(c):
        here = pl.ds(pl.multiple_of(c * wide, wide), wide)
        gamma = jnp.dot(weight[...], blocks[:, here], preferred_element_type=jnp.float32)
        for i in range(occ_g):
            for q in range(shards):
                low = i * virt + q * slab
                staged[q, i, :, here] = gamma[low:low + slab, :].astype(jnp.bfloat16)
        for q, z in enumerate(peers):
            out_copy(c, q, z, me_z).start()
        out_own(c).start()

    for copy in sent:
        copy.wait_send()

    @pl.loop(0, turns)
    def _(c):
        for q, z in enumerate(peers):
            out_copy(c, q, z, me_z).wait_send()
            out_copy(c, q, z, before[q]).wait_recv()
        out_own(c).wait()


def on_device(factors, screen, occ_energy, virt_energy):
    occ_g, virt, aux = factors.shape
    groups, shards = lax.axis_size("grp"), lax.axis_size("sh")
    rows = occ_g * virt
    piece = rows // 2
    share = piece // shards
    slab = virt // shards
    chips = groups // 2
    span = chips // 2
    pieces = 2 * groups
    wide = BLK * 4 if aux % (BLK * 4) == 0 else BLK
    turns = aux // wide
    wide_mask = jnp.repeat(jnp.repeat(screen, BLK, axis=1), BLK, axis=2)
    own_block = (factors * wide_mask.astype(jnp.bfloat16)).reshape(rows, aux)
    energy = virt_energy[None, :] - occ_energy[:, None]
    occ_own = lax.dynamic_slice_in_dim(occ_energy, lax.axis_index("grp") * occ_g, occ_g)
    own_energy = (virt_energy[None, :] - occ_own[:, None]).reshape(1, rows)
    all_energy = energy.reshape(pieces, shards, share, 1)
    dma = pltpu.SemaphoreType.DMA
    bf16 = jnp.bfloat16
    vmem = pl.BlockSpec(memory_space=pltpu.VMEM)
    return pl.pallas_call(
        functools.partial(amplitude_kernel, (occ_g, virt, aux, groups, shards)),
        out_shape=jax.ShapeDtypeStruct((occ_g, slab, aux * shards), bf16),
        in_specs=[pl.BlockSpec(memory_space=pl.ANY), vmem, vmem],
        out_specs=pl.BlockSpec(memory_space=pl.ANY),
        scratch_shapes=[
            pltpu.VMEM((groups * rows, aux), bf16),
            pltpu.VMEM((aux, rows), bf16),
            pltpu.VMEM((piece, rows), jnp.float32),
            pltpu.VMEM((pieces, shards, share, rows), bf16),
            pltpu.VMEM((pieces, shards - 1, share, rows), bf16),
            pltpu.VMEM((pieces, shards, share, rows), bf16),
            pltpu.VMEM((rows, rows), jnp.float32),
            pltpu.VMEM((rows, groups * rows), bf16),
            pltpu.VMEM((shards, occ_g, slab, aux), bf16),
            dma,
            dma((2, span, 2)),
            dma((2, span, 2)),
            dma((groups,)),
            dma((groups,)),
            dma((pieces, shards - 1)),
            dma((pieces, shards - 1)),
            dma((pieces, shards - 1)),
            dma((pieces, shards - 1)),
            dma((turns, shards - 1)),
            dma((turns, shards - 1)),
            dma((turns,)),
        ],
        cost_estimate=pl.CostEstimate(
            flops=4 * rows * groups * rows * aux, bytes_accessed=4 * rows * aux, transcendentals=0
        ),
        compiler_params=pltpu.CompilerParams(
            collective_id=0, has_side_effects=True, vmem_limit_bytes=56 * 1024 * 1024
        ),
    )(own_block, own_energy, all_energy)


def solution(mesh):
    placed = (P("grp", None, "sh"), P("grp", None, "sh"), P(), P())
    return jax.shard_map(
        on_device, mesh=mesh, in_specs=placed, out_specs=P("grp", "sh", None), check_vma=False
    )
```

time: 750 us -> 201 us (0.27)
  waiting for transfers between devices: 383 us -> 0 us
  blocking collectives: 202 us -> 0 us
  Pallas kernels: 0 us -> 188 us
  matrix products: 86.3 us -> 0 us
  local copies, waits for them, and re-layouts: 39.1 us -> 7.42 us
  other arithmetic: 23.7 us -> 5.65 us
  between operations: 13.5 us -> 0.02 us
    ppermute x7 -> x0, waiting for transfers between devices: 235 us -> none  [passed_along(): return lax.ppermute(value, axis, pairs)]
    pallas_call x0 -> x1, Pallas kernels: none -> 188 us  [on_device(): pl.pallas_call(functools.partial(amplitude_kernel, (occ_g, virt, aux, gro...]
    reduce_scatter x8 -> x0, waiting for transfers between devices: 147 us -> none  [update(): lax.psum_scatter(lax.dot_general(own_block, partner, (((1,), (1,)), ((),...]
    all_gather x8 -> x0, blocking collectives: 122 us -> none  [update(): full_amp = lax.all_gather(amplitude, 'sh', axis=0, tiled=True)]
    dot_general x16 -> x0, matrix products: 86.3 us -> none  [the longest x8 51.6 us: update(): jnp.dot(combined, partner, preferred_element_type=jnp.float32)]
    all_to_all x1 -> x0, blocking collectives: 80.5 us -> none  [on_device(): lax.all_to_all(gamma_local, 'sh', split_axis=1, concat_axis=2, tiled=True)]
    convert_element_type x24 -> x0, local copies, waits for them, and re-layouts: 19.3 us -> none  [the longest x16 17.3 us: update(): full_amp.reshape(occ_g, virt_width, occ_g, virt_width).astype(jnp.float32)]
    convert_element_type x18 -> x1, other arithmetic: 19.6 us -> 0.68 us  [on_device(): own_block = (factors * wide_mask.astype(jnp.bfloat16)).reshape(rows, aux)]
  transfers between devices with their start and end apart: 15 -> 0, of which waited for: 15 -> 0; matrix products, arithmetic and copies ran while one was open for 2% -> 0% of each run, Pallas kernels for 0% -> 0%
where the time goes in v1:
time: 201 us
  Pallas kernels  188 us (94%)
  local copies, waits for them, and re-layouts  7.42 us (4%)
  other arithmetic  5.65 us (3%)
    pallas_call x1, Pallas kernels, on_device(): pl.pallas_call(functools.partial(amplitude_kernel, (occ_g, virt, aux, gro...  188 us
    unnamed x5, local copies, waits for them, and re-layouts  4.13 us

profile of v1, /device:TPU:0, one launch (start us, length us, event | category | flops | bytes accessed | tf_op | source)
XLA Modules:
  0.0 200.9 jit_solution(5814701843143899131)
XLA Ops:
  0.0 0.7 dynamic_slice.3
  0.7 0.7 convert_element_type.11
  1.4 0.7 subtract_bitcast_fusion
  2.1 0.5 copy.13
  2.7 0.7 broadcast_subtract_fusion
  3.4 0.1 broadcast_bitcast_fusion
  3.5 2.6 %sub.54.all_energy = f32[16,4,48,1]{3,2,1,0:T(8,128)} reshape(f32[24,128]{1,0:T(8,128)S(1)} %broadcast_subtract_fusion) | data formatting | bytes 24576 | tf_op jit(solution)/shard_map/sub | solution.py:244
  6.1 3.5 %broadcast_multiply_fusion = bf16[3,128,3584]{2,1,0:T(8,128)(2,1)} fusion(bf16[3,128,3584]{2,1,0:T(8,128)(2,1)} %param.4, bf16[3,3584]{1,0:T(4,128)(2,1)S(1)} %bitcast.16), kind=kLoop, calls=%fused_computation | loop fusion | flops 1376256 | bytes 5526528 | tf_op jit(solution)/shard_map/mul | solution.py:243
  9.6 187.8 %shard_map.46 = bf16[3,32,14336]{2,1,0:T(8,128)(2,1)} custom-call(bf16[384,3584]{1,0:T(8,128)(2,1)} %bitcast.15, f32[1,384]{1,0:T(1,128)} %bitcast.18, f32[16,4,48,1]{3,2,1,0:T(8,128)} %sub.54.all_energy), custom_call_target="tpu_custom_call" | custom-call | flops 16911433728 | bytes 5505024 | tf_op jit(solution)/shard_map/pallas_call | solution.py:251
  197.4 3.5 %copy.16 = bf16[3,32,14336]{2,1,0:T(8,128)(2,1)} copy(bf16[3,32,14336]{2,1,0:T(8,128)(2,1)} %shard_map.46) | data formatting | bytes 5505024
  (2 shorter events, 0.0 us)

commit v2 on v1

v2 whole, which is shorter than its diff:
```python
import functools

import jax
import jax.numpy as jnp
from jax import lax
from jax.experimental import pallas as pl
from jax.experimental.pallas import tpu as pltpu
from jax.sharding import PartitionSpec as P

BLK = 128
PIECE = 64
WINDOW = 2
MESH = pl.DeviceIdType.MESH


def amplitude_kernel(
    dims, own_hbm, screen, occ_energy, virt_energy, out, blocks, own_t, part32, part16, arrived, amp, tile32, turned,
    energy, weight, staged, own_sem, ring_send, ring_recv, twin_send, twin_recv, part_send, part_recv, amp_send,
    amp_recv, out_send, out_recv, out_local,
):
    occ_g, virt, aux, groups, shards = dims
    rows = occ_g * virt
    per_block = rows // PIECE
    per_orbital = virt // PIECE
    share = PIECE // shards
    slab = virt // shards
    chips = groups // 2
    span = chips // 2
    rounds = per_block * (span - 1) + per_block // 2
    me_g, me_z = lax.axis_index("grp"), lax.axis_index("sh")
    core = lax.rem(me_g, 2)
    chip = lax.div(me_g, 2)
    odd, line = lax.rem(chip, 2), lax.div(chip, 2)
    spot = line + odd * (chips - 1 - 2 * line)

    def at(offset, other):
        place = lax.rem(spot + offset + chips, chips)
        that = 2 * place + lax.div(place, span) * (2 * chips - 1 - 4 * place)
        return 2 * that + (1 - core if other else core)

    def rows_of(offset, other, chunk):
        return pl.ds(pl.multiple_of((per_block * at(offset, other) + chunk) * PIECE, PIECE), PIECE)

    right, left, twin = at(1, False), at(-1, False), at(0, True)
    peers = [lax.rem(me_z + q, shards) for q in range(1, shards)]
    before = [lax.rem(me_z - q + shards, shards) for q in range(1, shards)]

    own_rows = pl.ds(pl.multiple_of(me_g * rows, rows), rows)
    load = pltpu.make_async_copy(own_hbm, blocks.at[own_rows], own_sem)
    load.start()
    barrier = pltpu.get_barrier_semaphore()
    for g in (right, left, twin):
        pl.semaphore_signal(barrier, inc=1, device_id=(g, me_z), device_id_type=MESH)
    for z in peers:
        pl.semaphore_signal(barrier, inc=1, device_id=(me_g, z), device_id_type=MESH)
    load.wait()

    @pl.loop(0, aux // BLK)
    def _(p):
        columns = pl.ds(pl.multiple_of(p * BLK, BLK), BLK)
        for i in range(occ_g):
            keep = screen[i, 0, p].astype(jnp.float32)
            here = pl.ds(pl.multiple_of(me_g * rows + i * virt, virt), virt)
            blocks[here, columns] = (blocks[here, columns].astype(jnp.float32) * keep).astype(jnp.bfloat16)

    pl.semaphore_wait(barrier, 3 + shards - 1)

    sent = []

    def started(copy):
        copy.start()
        return copy

    def go(copy):
        sent.append(started(copy))

    def place_of(way, turn):
        step, rank = turn // per_block + 1, turn % per_block
        return step, (rank if way == 0 else per_block - 1 - rank)

    def ring(way, turn, receiving):
        step, chunk = place_of(way, turn)
        back = step if receiving else step - 1
        where = rows_of(-back if way == 0 else back, False, chunk)
        return pltpu.make_async_remote_copy(
            src_ref=blocks.at[where], dst_ref=blocks.at[where],
            send_sem=ring_send.at[way, turn], recv_sem=ring_recv.at[way, turn],
            device_id=(right if way == 0 else left, me_z), device_id_type=MESH,
        )

    def to_twin(offset, other, chunk, index):
        where = rows_of(offset, other, chunk)
        return pltpu.make_async_remote_copy(
            src_ref=blocks.at[where], dst_ref=blocks.at[where],
            send_sem=twin_send.at[index], recv_sem=twin_recv.at[index],
            device_id=(twin, me_z), device_id_type=MESH,
        )

    flying = {}
    for turn in range(min(WINDOW, rounds)):
        flying[turn] = [started(ring(way, turn, False)) for way in (0, 1)]
    for chunk in range(per_block):
        go(to_twin(0, False, chunk, chunk))

    depth = BLK * 4 if aux % (BLK * 4) == 0 else BLK

    @pl.loop(0, aux // depth)
    def _(k):
        at_k = pl.ds(pl.multiple_of(k * depth, depth), depth)
        own_t[at_k, :] = blocks[own_rows, at_k].astype(jnp.float32).T.astype(jnp.bfloat16)

    turned[...] = jnp.broadcast_to(virt_energy[...], (virt, virt)).T

    @pl.loop(0, groups * occ_g)
    def _(j):
        for part in range(per_orbital):
            for q in range(shards):
                low = part * PIECE + q * share
                energy[j * per_orbital + part, q] = turned[low:low + share, :] - occ_energy[j]

    own_energy = jnp.concatenate([virt_energy[...] - occ_energy[me_g * occ_g + i] for i in range(occ_g)], axis=1)

    def product(batch, number):
        part32[...] = jnp.zeros_like(part32)

        @pl.loop(0, aux // depth)
        def _(k):
            at_k = pl.ds(pl.multiple_of(k * depth, depth), depth)
            left_side = jnp.concatenate([blocks[rows_of(*entry), at_k] for entry in batch], axis=0)
            part32[...] += jnp.dot(left_side, own_t[at_k, :], preferred_element_type=jnp.float32)

        for c in range(len(batch)):
            for q in range(shards):
                low = c * PIECE + q * share
                part16[number, q, c] = part32[low:low + share, :].astype(jnp.bfloat16)
        for q, z in enumerate(peers):
            go(pltpu.make_async_remote_copy(
                src_ref=part16.at[number, z], dst_ref=arrived.at[number, q],
                send_sem=part_send.at[number, q], recv_sem=part_recv.at[number, q],
                device_id=(me_g, z), device_id_type=MESH,
            ))

    def divide(batch, number):
        for q in range(shards - 1):
            pltpu.make_async_copy(arrived.at[number, q], arrived.at[number, q], part_recv.at[number, q]).wait()
        for c, (offset, other, chunk) in enumerate(batch):
            total = part16[number, me_z, c].astype(jnp.float32)
            for q in range(shards - 1):
                total += arrived[number, q, c].astype(jnp.float32)
            theirs = energy[per_block * at(offset, other) + chunk, me_z]
            gap = jnp.concatenate([theirs] * occ_g, axis=1) + own_energy
            amp[number, me_z, c] = (total / gap).astype(jnp.bfloat16)
        for q, z in enumerate(peers):
            go(pltpu.make_async_remote_copy(
                src_ref=amp.at[number, me_z], dst_ref=amp.at[number, me_z],
                send_sem=amp_send.at[number, q], recv_sem=amp_recv.at[number, q],
                device_id=(me_g, z), device_id_type=MESH,
            ))

    seen = {}

    def combine(batch, number):
        for q, z in enumerate(before):
            slot = amp.at[number, z]
            pltpu.make_async_copy(slot, slot, amp_recv.at[number, q]).wait()
        for c, (offset, other, chunk) in enumerate(batch):
            j = chunk // per_orbital
            key = (offset % chips, other, j)
            seen.setdefault(key, {})[chunk % per_orbital] = (number, c)
            if len(seen[key]) < per_orbital:
                continue
            for part, (n, at_c) in seen[key].items():
                for q in range(shards):
                    low = part * PIECE + q * share
                    tile32[low:low + share, :] = amp[n, q, at_c].astype(jnp.float32)
            columns = pl.ds(pl.multiple_of(at(offset, other) * rows + j * virt, virt), virt)
            for i in range(occ_g):
                tile = tile32[:, i * virt:(i + 1) * virt]
                weight[i * virt:(i + 1) * virt, columns] = (2.0 * tile.T - tile).astype(jnp.bfloat16)

    home = [(0, False, c) for c in range(per_block)] + [(0, True, c) for c in range(per_block)]
    batches = [home[b:b + 4] for b in range(0, len(home), 4)]
    first = len(batches)
    for number, batch in enumerate(batches):
        for offset, other, chunk in batch:
            if other:
                to_twin(0, True, chunk, chunk).wait_recv()
        product(batch, number)
        if number >= 1:
            divide(batches[number - 1], number - 1)
        if number >= 2:
            combine(batches[number - 2], number - 2)
    for turn in range(rounds):
        number = first + turn
        batch = []
        for way in (0, 1):
            step, chunk = place_of(way, turn)
            batch.append((-step if way == 0 else step, False, chunk))
        for way in (0, 1):
            ring(way, turn, True).wait_recv()
            go(to_twin(*batch[way], per_block + 2 * turn + way))
        for copy in flying[turn]:
            copy.wait_send()
        if turn + WINDOW < rounds:
            flying[turn + WINDOW] = [started(ring(way, turn + WINDOW, False)) for way in (0, 1)]
        divide(batches[number - 1], number - 1)
        for way in (0, 1):
            offset, _, chunk = batch[way]
            to_twin(offset, True, chunk, per_block + 2 * turn + way).wait_recv()
        batch = batch + [(offset, True, chunk) for offset, _, chunk in batch]
        batches.append(batch)
        product(batch, number)
        if number >= 2:
            combine(batches[number - 2], number - 2)
    last = len(batches) - 1
    divide(batches[last], last)
    combine(batches[last - 1], last - 1)
    combine(batches[last], last)

    wide = depth
    turns = aux // wide

    def out_copy(c, q, z, source):
        return pltpu.make_async_remote_copy(
            src_ref=staged.at[z, :, :, pl.ds(pl.multiple_of(c * wide, wide), wide)],
            dst_ref=out.at[:, :, pl.ds(pl.multiple_of(source * aux + c * wide, wide), wide)],
            send_sem=out_send.at[c, q], recv_sem=out_recv.at[c, q],
            device_id=(me_g, z), device_id_type=MESH,
        )

    def out_own(c):
        return pltpu.make_async_copy(
            staged.at[me_z, :, :, pl.ds(pl.multiple_of(c * wide, wide), wide)],
            out.at[:, :, pl.ds(pl.multiple_of(me_z * aux + c * wide, wide), wide)],
            out_local.at[c],
        )

    @pl.loop(0, turns)
    def _(c):
        here = pl.ds(pl.multiple_of(c * wide, wide), wide)
        gamma = jnp.dot(weight[...], blocks[:, here], preferred_element_type=jnp.float32)
        for i in range(occ_g):
            for q in range(shards):
                low = i * virt + q * slab
                staged[q, i, :, here] = gamma[low:low + slab, :].astype(jnp.bfloat16)
        for q, z in enumerate(peers):
            out_copy(c, q, z, me_z).start()
        out_own(c).start()

    for copy in sent:
        copy.wait_send()

    @pl.loop(0, turns)
    def _(c):
        for q, z in enumerate(peers):
            out_copy(c, q, z, me_z).wait_send()
            out_copy(c, q, z, before[q]).wait_recv()
        out_own(c).wait()


def on_device(factors, screen, occ_energy, virt_energy):
    occ_g, virt, aux = factors.shape
    groups, shards = lax.axis_size("grp"), lax.axis_size("sh")
    rows = occ_g * virt
    per_block = rows // PIECE
    share = PIECE // shards
    slab = virt // shards
    span = groups // 4
    rounds = per_block * (span - 1) + per_block // 2
    batches = groups * per_block // 4
    turns = aux // (BLK * 4 if aux % (BLK * 4) == 0 else BLK)
    dma = pltpu.SemaphoreType.DMA
    bf16 = jnp.bfloat16
    smem = pl.BlockSpec(memory_space=pltpu.SMEM)
    return pl.pallas_call(
        functools.partial(amplitude_kernel, (occ_g, virt, aux, groups, shards)),
        out_shape=jax.ShapeDtypeStruct((occ_g, slab, aux * shards), bf16),
        in_specs=[pl.BlockSpec(memory_space=pl.ANY), smem, smem, pl.BlockSpec(memory_space=pltpu.VMEM)],
        out_specs=pl.BlockSpec(memory_space=pl.ANY),
        scratch_shapes=[
            pltpu.VMEM((groups * rows, aux), bf16),
            pltpu.VMEM((aux, rows), bf16),
            pltpu.VMEM((4 * PIECE, rows), jnp.float32),
            pltpu.VMEM((batches, shards, 4, share, rows), bf16),
            pltpu.VMEM((batches, shards - 1, 4, share, rows), bf16),
            pltpu.VMEM((batches, shards, 4, share, rows), bf16),
            pltpu.VMEM((virt, rows), jnp.float32),
            pltpu.VMEM((virt, virt), jnp.float32),
            pltpu.VMEM((groups * per_block, shards, share, virt), jnp.float32),
            pltpu.VMEM((rows, groups * rows), bf16),
            pltpu.VMEM((shards, occ_g, slab, aux), bf16),
            dma,
            dma((2, rounds)),
            dma((2, rounds)),
            dma((groups * per_block // 2,)),
            dma((groups * per_block // 2,)),
            dma((batches, shards - 1)),
            dma((batches, shards - 1)),
            dma((batches, shards - 1)),
            dma((batches, shards - 1)),
            dma((turns, shards - 1)),
            dma((turns, shards - 1)),
            dma((turns,)),
        ],
        cost_estimate=pl.CostEstimate(
            flops=4 * rows * groups * rows * aux, bytes_accessed=4 * rows * aux, transcendentals=0
        ),
        compiler_params=pltpu.CompilerParams(
            collective_id=0, has_side_effects=True, vmem_limit_bytes=56 * 1024 * 1024
        ),
    )(factors.reshape(rows, aux), screen, occ_energy, virt_energy.reshape(1, virt))


def solution(mesh):
    placed = (P("grp", None, "sh"), P("grp", None, "sh"), P(), P())
    return jax.shard_map(
        on_device, mesh=mesh, in_specs=placed, out_specs=P("grp", "sh", None), check_vma=False
    )
```

time: 201 us -> 185 us (0.920)
  Pallas kernels: 188 us -> 180 us
  other arithmetic: 5.65 us -> 0 us
  local copies, waits for them, and re-layouts: 7.42 us -> 3.49 us
    pallas_call x1, Pallas kernels: 188 us -> 180 us  [on_device(): pl.pallas_call(functools.partial(amplitude_kernel, (occ_g, virt, aux, gro...]
    mul x1 -> x0, other arithmetic: 3.5 us -> none  [on_device(): own_block = (factors * wide_mask.astype(jnp.bfloat16)).reshape(rows, aux)]
    sub x1 -> x0, local copies, waits for them, and re-layouts: 2.56 us -> none  [on_device(): energy = virt_energy[None, :] - occ_energy[:, None]]
    unnamed x5 -> x1, local copies, waits for them, and re-layouts: 4.13 us -> 3.49 us
where the time goes in v2:
time: 185 us; the launch traced here: 184 us
  Pallas kernels  180 us (97%)
  local copies, waits for them, and re-layouts  3.49 us (2%)
    pallas_call x1, Pallas kernels, on_device(): pl.pallas_call(functools.partial(amplitude_kernel, (occ_g, virt, aux, gro...  180 us

profile of v2, /device:TPU:0, one launch (start us, length us, event | category | flops | bytes accessed | tf_op | source)
XLA Modules:
  0.0 184.0 jit_solution(8593576286448482452)
XLA Ops:
  0.0 180.5 %shard_map.46 = bf16[3,32,14336]{2,1,0:T(8,128)(2,1)} custom-call(bf16[384,3584]{1,0:T(8,128)(2,1)} %bitcast.2, s32[3,1,28]{2,1,0:T(1,128)} %screen.1, f32[24]{0:T(128)} %occ_energy.1, f32[1,128]{1,0:T(1,128)} %bitcast.3), custom_call_target="tpu_custom_call" | custom-call | flops 16911433728 | bytes 5505024 | tf_op jit(solution)/shard_map/pallas_call | solution.py:275
  180.5 3.5 %copy.6 = bf16[3,32,14336]{2,1,0:T(8,128)(2,1)} copy(bf16[3,32,14336]{2,1,0:T(8,128)(2,1)} %shard_map.46) | data formatting | bytes 5505024

commit v3 on v2

--- a/solution.py
+++ b/solution.py
@@ -9,12 +9,12 @@
 
 BLK = 128
 PIECE = 64
-WINDOW = 2
+WINDOW = 3
 MESH = pl.DeviceIdType.MESH
 
 
 def amplitude_kernel(
-    dims, own_hbm, screen, occ_energy, virt_energy, out, blocks, own_t, part32, part16, arrived, amp, tile32, turned,
+    dims, own_hbm, screen, occ_energy, virt_energy, out, blocks, own_t, part32, part16, arrived, sums, amp, tile32, turned,
     energy, weight, staged, own_sem, ring_send, ring_recv, twin_send, twin_recv, part_send, part_recv, amp_send,
     amp_recv, out_send, out_recv, out_local,
 ):
@@ -27,6 +27,7 @@
     chips = groups // 2
     span = chips // 2
     rounds = per_block * (span - 1) + per_block // 2
+    levels = shards.bit_length() - 1
     me_g, me_z = lax.axis_index("grp"), lax.axis_index("sh")
     core = lax.rem(me_g, 2)
     chip = lax.div(me_g, 2)
@@ -133,36 +134,75 @@
             for q in range(shards):
                 low = c * PIECE + q * share
                 part16[number, q, c] = part32[low:low + share, :].astype(jnp.bfloat16)
-        for q, z in enumerate(peers):
-            go(pltpu.make_async_remote_copy(
-                src_ref=part16.at[number, z], dst_ref=arrived.at[number, q],
-                send_sem=part_send.at[number, q], recv_sem=part_recv.at[number, q],
-                device_id=(me_g, z), device_id_type=MESH,
-            ))
+        halve(number, 0, part16, 0)
+
+    bits = [lax.rem(lax.div(me_z, 1 << s), 2) for s in range(levels)]
+    start = [0]
+    for s in range(levels):
+        start.append(start[s] + bits[s] * (shards >> (s + 1)))
+    mine = start[levels]
+    partner = [me_z + (1 - 2 * bits[s]) * (1 << s) for s in range(levels)]
+    room = [shards - (shards >> s) for s in range(levels)]
+
+    def halve(number, s, source, base):
+        length = shards >> (s + 1)
+        go(pltpu.make_async_remote_copy(
+            src_ref=source.at[number, pl.ds(base + (1 - bits[s]) * length, length)],
+            dst_ref=arrived.at[number, pl.ds(room[s], length)],
+            send_sem=part_send.at[number, s], recv_sem=part_recv.at[number, s],
+            device_id=(me_g, partner[s]), device_id_type=MESH,
+        ))
+
+    def halved(number, s):
+        length = shards >> (s + 1)
+        slot = arrived.at[number, pl.ds(room[s], length)]
+        pltpu.make_async_copy(slot, slot, part_recv.at[number, s]).wait()
+        source, base = (part16, 0) if s == 0 else (sums, room[s - 1])
+        kept = source[number, pl.ds(base + bits[s] * length, length)].astype(jnp.float32)
+        return kept + arrived[number, room[s]:room[s] + length].astype(jnp.float32)
+
+    def double(number, s):
+        held = amp.at[number, pl.ds(start[s + 1], shards >> (s + 1))]
+        go(pltpu.make_async_remote_copy(
+            src_ref=held, dst_ref=held, send_sem=amp_send.at[number, s], recv_sem=amp_recv.at[number, s],
+            device_id=(me_g, partner[s]), device_id_type=MESH,
+        ))
+
+    def doubled(number, s):
+        length = shards >> (s + 1)
+        slot = amp.at[number, pl.ds(start[s] + (1 - bits[s]) * length, length)]
+        pltpu.make_async_copy(slot, slot, amp_recv.at[number, s]).wait()
 
     def divide(batch, number):
-        for q in range(shards - 1):
-            pltpu.make_async_copy(arrived.at[number, q], arrived.at[number, q], part_recv.at[number, q]).wait()
+        total = halved(number, levels - 1)
         for c, (offset, other, chunk) in enumerate(batch):
-            total = part16[number, me_z, c].astype(jnp.float32)
-            for q in range(shards - 1):
-                total += arrived[number, q, c].astype(jnp.float32)
-            theirs = energy[per_block * at(offset, other) + chunk, me_z]
+            theirs = energy[per_block * at(offset, other) + chunk, mine]
             gap = jnp.concatenate([theirs] * occ_g, axis=1) + own_energy
-            amp[number, me_z, c] = (total / gap).astype(jnp.bfloat16)
-        for q, z in enumerate(peers):
-            go(pltpu.make_async_remote_copy(
-                src_ref=amp.at[number, me_z], dst_ref=amp.at[number, me_z],
-                send_sem=amp_send.at[number, q], recv_sem=amp_recv.at[number, q],
-                device_id=(me_g, z), device_id_type=MESH,
-            ))
+            amp[number, mine, c] = (total[0, c] / gap).astype(jnp.bfloat16)
+        double(number, levels - 1)
+
+    def stage(k, number):
+        if k < levels:
+            total = halved(number, k - 1)
+            sums[number, room[k - 1]:room[k - 1] + (shards >> k)] = total.astype(jnp.bfloat16)
+            halve(number, k, sums, room[k - 1])
+        elif k == levels:
+            divide(batches[number], number)
+        else:
+            doubled(number, 2 * levels - k)
+            if k < 2 * levels:
+                double(number, 2 * levels - k - 1)
+            else:
+                combine(batches[number], number)
+
+    def tick(time):
+        for k in range(2 * levels, 0, -1):
+            if (time - k) % 2 == 0 and 0 <= time - k < 2 * len(batches):
+                stage(k, (time - k) // 2)
 
     seen = {}
 
     def combine(batch, number):
-        for q, z in enumerate(before):
-            slot = amp.at[number, z]
-            pltpu.make_async_copy(slot, slot, amp_recv.at[number, q]).wait()
         for c, (offset, other, chunk) in enumerate(batch):
             j = chunk // per_orbital
             key = (offset % chips, other, j)
@@ -179,17 +219,17 @@
                 weight[i * virt:(i + 1) * virt, columns] = (2.0 * tile.T - tile).astype(jnp.bfloat16)
 
     home = [(0, False, c) for c in range(per_block)] + [(0, True, c) for c in range(per_block)]
-    batches = [home[b:b + 4] for b in range(0, len(home), 4)]
-    first = len(batches)
-    for number, batch in enumerate(batches):
+    first = len(home) // 4
+    batches = []
+    for number in range(first):
+        batch = home[4 * number:4 * number + 4]
         for offset, other, chunk in batch:
             if other:
                 to_twin(0, True, chunk, chunk).wait_recv()
+        batches.append(batch)
+        tick(2 * number)
         product(batch, number)
-        if number >= 1:
-            divide(batches[number - 1], number - 1)
-        if number >= 2:
-            combine(batches[number - 2], number - 2)
+        tick(2 * number + 1)
     for turn in range(rounds):
         number = first + turn
         batch = []
@@ -203,19 +243,16 @@
             copy.wait_send()
         if turn + WINDOW < rounds:
             flying[turn + WINDOW] = [started(ring(way, turn + WINDOW, False)) for way in (0, 1)]
-        divide(batches[number - 1], number - 1)
+        tick(2 * number)
         for way in (0, 1):
             offset, _, chunk = batch[way]
             to_twin(offset, True, chunk, per_block + 2 * turn + way).wait_recv()
         batch = batch + [(offset, True, chunk) for offset, _, chunk in batch]
         batches.append(batch)
         product(batch, number)
-        if number >= 2:
-            combine(batches[number - 2], number - 2)
-    last = len(batches) - 1
-    divide(batches[last], last)
-    combine(batches[last - 1], last - 1)
-    combine(batches[last], last)
+        tick(2 * number + 1)
+    for time in range(2 * len(batches), 2 * len(batches) + 2 * levels - 1):
+        tick(time)
 
     wide = depth
     turns = aux // wide
@@ -267,6 +304,7 @@
     slab = virt // shards
     span = groups // 4
     rounds = per_block * (span - 1) + per_block // 2
+    levels = shards.bit_length() - 1
     batches = groups * per_block // 4
     turns = aux // (BLK * 4 if aux % (BLK * 4) == 0 else BLK)
     dma = pltpu.SemaphoreType.DMA
@@ -283,6 +321,7 @@
             pltpu.VMEM((4 * PIECE, rows), jnp.float32),
             pltpu.VMEM((batches, shards, 4, share, rows), bf16),
             pltpu.VMEM((batches, shards - 1, 4, share, rows), bf16),
+            pltpu.VMEM((batches, shards - 1, 4, share, rows), bf16),
             pltpu.VMEM((batches, shards, 4, share, rows), bf16),
             pltpu.VMEM((virt, rows), jnp.float32),
             pltpu.VMEM((virt, virt), jnp.float32),
@@ -294,10 +333,10 @@
             dma((2, rounds)),
             dma((groups * per_block // 2,)),
             dma((groups * per_block // 2,)),
-            dma((batches, shards - 1)),
-            dma((batches, shards - 1)),
-            dma((batches, shards - 1)),
-            dma((batches, shards - 1)),
+            dma((batches, levels)),
+            dma((batches, levels)),
+            dma((batches, levels)),
+            dma((batches, levels)),
             dma((turns, shards - 1)),
             dma((turns, shards - 1)),
             dma((turns,)),

time: 185 us -> 203 us (1.097)
  Pallas kernels: 180 us -> 196 us
    pallas_call x1, Pallas kernels: 180 us -> 196 us  [on_device(): pl.pallas_call(functools.partial(amplitude_kernel, (occ_g, virt, aux, gro...]
where the time goes in v3:
time: 203 us; the launch traced here: 200 us
  Pallas kernels  196 us (97%)
  local copies, waits for them, and re-layouts  3.49 us (2%)
    pallas_call x1, Pallas kernels, on_device(): pl.pallas_call(functools.partial(amplitude_kernel, (occ_g, virt, aux, gro...  196 us

profile of v3, /device:TPU:0, one launch (start us, length us, event | category | flops | bytes accessed | tf_op | source)
XLA Modules:
  0.0 200.0 jit_solution(873922812591986762)
XLA Ops:
  0.0 196.5 %shard_map.46 = bf16[3,32,14336]{2,1,0:T(8,128)(2,1)} custom-call(bf16[384,3584]{1,0:T(8,128)(2,1)} %bitcast.2, s32[3,1,28]{2,1,0:T(1,128)} %screen.1, f32[24]{0:T(128)} %occ_energy.1, f32[1,128]{1,0:T(1,128)} %bitcast.3), custom_call_target="tpu_custom_call" | custom-call | flops 16911433728 | bytes 5505024 | tf_op jit(solution)/shard_map/pallas_call | solution.py:313
  196.5 3.5 %copy.6 = bf16[3,32,14336]{2,1,0:T(8,128)(2,1)} copy(bf16[3,32,14336]{2,1,0:T(8,128)(2,1)} %shard_map.46) | data formatting | bytes 5505024

commit v4 on v2

--- a/solution.py
+++ b/solution.py
@@ -9,7 +9,7 @@
 
 BLK = 128
 PIECE = 64
-WINDOW = 2
+WINDOW = 4
 MESH = pl.DeviceIdType.MESH
 
 
@@ -217,7 +217,7 @@
     combine(batches[last - 1], last - 1)
     combine(batches[last], last)
 
-    wide = depth
+    wide = BLK * 2 if aux % (BLK * 2) == 0 else BLK
     turns = aux // wide
 
     def out_copy(c, q, z, source):
@@ -268,7 +268,7 @@
     span = groups // 4
     rounds = per_block * (span - 1) + per_block // 2
     batches = groups * per_block // 4
-    turns = aux // (BLK * 4 if aux % (BLK * 4) == 0 else BLK)
+    turns = aux // (BLK * 2 if aux % (BLK * 2) == 0 else BLK)
     dma = pltpu.SemaphoreType.DMA
     bf16 = jnp.bfloat16
     smem = pl.BlockSpec(memory_space=pltpu.SMEM)

time: 185 us -> 186 us (level)
  Pallas kernels: 180 us -> 182 us
    pallas_call x1, Pallas kernels: 180 us -> 182 us  [on_device(): pl.pallas_call(functools.partial(amplitude_kernel, (occ_g, virt, aux, gro...]
where the time goes in v4:
time: 186 us
  Pallas kernels  182 us (98%)
  local copies, waits for them, and re-layouts  3.49 us (2%)
    pallas_call x1, Pallas kernels, on_device(): pl.pallas_call(functools.partial(amplitude_kernel, (occ_g, virt, aux, gro...  182 us

profile of v4, /device:TPU:0, one launch (start us, length us, event | category | flops | bytes accessed | tf_op | source)
XLA Modules:
  0.0 185.9 jit_solution(13839063060743890806)
XLA Ops:
  0.0 182.4 %shard_map.46 = bf16[3,32,14336]{2,1,0:T(8,128)(2,1)} custom-call(bf16[384,3584]{1,0:T(8,128)(2,1)} %bitcast.2, s32[3,1,28]{2,1,0:T(1,128)} %screen.1, f32[24]{0:T(128)} %occ_energy.1, f32[1,128]{1,0:T(1,128)} %bitcast.3), custom_call_target="tpu_custom_call" | custom-call | flops 16911433728 | bytes 5505024 | tf_op jit(solution)/shard_map/pallas_call | solution.py:275
  182.4 3.5 %copy.6 = bf16[3,32,14336]{2,1,0:T(8,128)(2,1)} copy(bf16[3,32,14336]{2,1,0:T(8,128)(2,1)} %shard_map.46) | data formatting | bytes 5505024

commit v5 on v2

--- a/solution.py
+++ b/solution.py
@@ -9,7 +9,7 @@
 
 BLK = 128
 PIECE = 64
-WINDOW = 2
+WINDOW = 3
 MESH = pl.DeviceIdType.MESH
 
 
@@ -46,23 +46,33 @@
     before = [lax.rem(me_z - q + shards, shards) for q in range(1, shards)]
 
     own_rows = pl.ds(pl.multiple_of(me_g * rows, rows), rows)
-    load = pltpu.make_async_copy(own_hbm, blocks.at[own_rows], own_sem)
-    load.start()
+    order = [c for pair in zip(range(per_block // 2), range(per_block - 1, -1, -1)) for c in pair]
+
+    def load(chunk):
+        return pltpu.make_async_copy(
+            own_hbm.at[pl.ds(chunk * PIECE, PIECE)], blocks.at[rows_of(0, False, chunk)], own_sem.at[chunk]
+        )
+
+    for chunk in order:
+        load(chunk).start()
     barrier = pltpu.get_barrier_semaphore()
     for g in (right, left, twin):
         pl.semaphore_signal(barrier, inc=1, device_id=(g, me_z), device_id_type=MESH)
     for z in peers:
         pl.semaphore_signal(barrier, inc=1, device_id=(me_g, z), device_id_type=MESH)
-    load.wait()
-
-    @pl.loop(0, aux // BLK)
-    def _(p):
-        columns = pl.ds(pl.multiple_of(p * BLK, BLK), BLK)
-        for i in range(occ_g):
-            keep = screen[i, 0, p].astype(jnp.float32)
-            here = pl.ds(pl.multiple_of(me_g * rows + i * virt, virt), virt)
+
+    def masked(chunk):
+        load(chunk).wait()
+
+        @pl.loop(0, aux // BLK)
+        def _(p):
+            columns = pl.ds(pl.multiple_of(p * BLK, BLK), BLK)
+            keep = screen[chunk // per_orbital, 0, p].astype(jnp.float32)
+            here = rows_of(0, False, chunk)
             blocks[here, columns] = (blocks[here, columns].astype(jnp.float32) * keep).astype(jnp.bfloat16)
 
+    for chunk in order[:2]:
+        masked(chunk)
     pl.semaphore_wait(barrier, 3 + shards - 1)
 
     sent = []
@@ -97,8 +107,12 @@
         )
 
     flying = {}
-    for turn in range(min(WINDOW, rounds)):
-        flying[turn] = [started(ring(way, turn, False)) for way in (0, 1)]
+    for turn in range(per_block):
+        if turn >= 1 and 2 * turn < per_block:
+            masked(order[2 * turn])
+            masked(order[2 * turn + 1])
+        if turn < min(WINDOW, rounds):
+            flying[turn] = [started(ring(way, turn, False)) for way in (0, 1)]
     for chunk in range(per_block):
         go(to_twin(0, False, chunk, chunk))
 
@@ -213,8 +227,8 @@
         if number >= 2:
             combine(batches[number - 2], number - 2)
     last = len(batches) - 1
+    combine(batches[last - 1], last - 1)
     divide(batches[last], last)
-    combine(batches[last - 1], last - 1)
     combine(batches[last], last)
 
     wide = depth
@@ -289,7 +303,7 @@
             pltpu.VMEM((groups * per_block, shards, share, virt), jnp.float32),
             pltpu.VMEM((rows, groups * rows), bf16),
             pltpu.VMEM((shards, occ_g, slab, aux), bf16),
-            dma,
+            dma((per_block,)),
             dma((2, rounds)),
             dma((2, rounds)),
             dma((groups * per_block // 2,)),

time: 185 us -> 185 us (level); the launches traced: 184 us -> 181 us
  Pallas kernels: 180 us -> 178 us
    pallas_call x1, Pallas kernels: 180 us -> 178 us  [on_device(): pl.pallas_call(functools.partial(amplitude_kernel, (occ_g, virt, aux, gro...]
where the time goes in v5:
time: 185 us; the launch traced here: 181 us
  Pallas kernels  178 us (96%)
  local copies, waits for them, and re-layouts  3.49 us (2%)
    pallas_call x1, Pallas kernels, on_device(): pl.pallas_call(functools.partial(amplitude_kernel, (occ_g, virt, aux, gro...  178 us

profile of v5, /device:TPU:0, one launch (start us, length us, event | category | flops | bytes accessed | tf_op | source)
XLA Modules:
  0.0 181.1 jit_solution(5680727336367870144)
XLA Ops:
  0.0 177.6 %shard_map.46 = bf16[3,32,14336]{2,1,0:T(8,128)(2,1)} custom-call(bf16[384,3584]{1,0:T(8,128)(2,1)} %bitcast.2, s32[3,1,28]{2,1,0:T(1,128)} %screen.1, f32[24]{0:T(128)} %occ_energy.1, f32[1,128]{1,0:T(1,128)} %bitcast.3), custom_call_target="tpu_custom_call" | custom-call | flops 16911433728 | bytes 5505024 | tf_op jit(solution)/shard_map/pallas_call | solution.py:289
  177.6 3.5 %copy.6 = bf16[3,32,14336]{2,1,0:T(8,128)(2,1)} copy(bf16[3,32,14336]{2,1,0:T(8,128)(2,1)} %shard_map.46) | data formatting | bytes 5505024

commit v6 on v5

--- a/solution.py
+++ b/solution.py
@@ -217,13 +217,13 @@
             copy.wait_send()
         if turn + WINDOW < rounds:
             flying[turn + WINDOW] = [started(ring(way, turn + WINDOW, False)) for way in (0, 1)]
-        divide(batches[number - 1], number - 1)
         for way in (0, 1):
             offset, _, chunk = batch[way]
             to_twin(offset, True, chunk, per_block + 2 * turn + way).wait_recv()
         batch = batch + [(offset, True, chunk) for offset, _, chunk in batch]
         batches.append(batch)
         product(batch, number)
+        divide(batches[number - 1], number - 1)
         if number >= 2:
             combine(batches[number - 2], number - 2)
     last = len(batches) - 1

time: 185 us -> 183 us (0.989); the launches traced: 181 us -> 183 us
  Pallas kernels: 178 us -> 180 us
    pallas_call x1, Pallas kernels: 178 us -> 180 us  [on_device(): pl.pallas_call(functools.partial(amplitude_kernel, (occ_g, virt, aux, gro...]
where the time goes in v6:
time: 183 us
  Pallas kernels  180 us (98%)
  local copies, waits for them, and re-layouts  3.49 us (2%)
    pallas_call x1, Pallas kernels, on_device(): pl.pallas_call(functools.partial(amplitude_kernel, (occ_g, virt, aux, gro...  180 us

profile of v6, /device:TPU:0, one launch (start us, length us, event | category | flops | bytes accessed | tf_op | source)
XLA Modules:
  0.0 183.3 jit_solution(8486094405556558958)
XLA Ops:
  0.0 179.8 %shard_map.46 = bf16[3,32,14336]{2,1,0:T(8,128)(2,1)} custom-call(bf16[384,3584]{1,0:T(8,128)(2,1)} %bitcast.2, s32[3,1,28]{2,1,0:T(1,128)} %screen.1, f32[24]{0:T(128)} %occ_energy.1, f32[1,128]{1,0:T(1,128)} %bitcast.3), custom_call_target="tpu_custom_call" | custom-call | flops 16911433728 | bytes 5505024 | tf_op jit(solution)/shard_map/pallas_call | solution.py:289
  179.8 3.5 %copy.6 = bf16[3,32,14336]{2,1,0:T(8,128)(2,1)} copy(bf16[3,32,14336]{2,1,0:T(8,128)(2,1)} %shard_map.46) | data formatting | bytes 5505024
